TPU v7x, 32 devices: a whole 2x2x4 slice. The times are simulated.
32 devices in a mesh: space: 8 (over z, x), rep: 4 (over y, core).
Axes of the slice: x: 2, y: 2, z: 4, core: 2. Of those that a mesh axis runs over, the one named last changes fastest.
Arguments:
- voxels: bfloat16 [4, 32, 512, 128], P('rep', 'space'), may hold values from -6 to 6
- occupied: int32 [4, 32], P('rep', 'space'), may hold values from 0 to 1, as said below
- neighbours: int32 [4, 32, 6], P('rep', 'space'), may hold values from -1 to 31, as said below
- first_weight: bfloat16 [27, 128, 128], replicated, may hold values from -0.109375 to 0.109375
- second_weight: bfloat16 [27, 128, 128], replicated, may hold values from -0.109375 to 0.109375
- cotangent: bfloat16 [4, 32, 512, 128], P('rep', 'space'), may hold values from -0.0234375 to 0.0234375
Outputs:
- output_field: bfloat16 [4, 32, 512, 128], P('rep', 'space')
- first_grad: float32 [27, 128, 128], replicated
- second_grad: float32 [27, 128, 128], replicated
Inputs may be any that keep to these rules, and one draw needn't show every extreme that they name: In every slab each device of space holds n blocks in its first n slots (occupied 1) and padding after them, n from 1 to 4; in some slab the last device holds 4. `neighbours`: device s of space owns one tile of 2 x 2 x 1 block positions. With h = log2(8) - 1, bit h of s is the tile's third coordinate (the slab is two tiles deep in the third dimension), and below it bit 2k of s is bit k of the tile's first coordinate and bit 2k+1 of s bit k of its second. Entry f names owner * 4 + slot of the occupied block of the same slab across face f (-x, +x, -y, +y, -z, +z), or -1 where there is none or the slot is padding; if a names b across face f, b names a across the opposite face.
All inputs are finite; a program needn't handle non-finite values.
Results may differ from a plain program's by a relative error of at most 0.0031.
Values may be sent and summed in bfloat16 or wider, within the bound.
A program may use at most 128 MiB of HBM per device.

v0:
```python
import functools

import jax
import jax.numpy as jnp
from jax import lax
from jax.experimental import pallas as pl
from jax.experimental.pallas import tpu as pltpu
from jax.sharding import PartitionSpec as P

MESH = pl.DeviceIdType.MESH
OPP = (1, 0, 3, 2, 5, 4)
F32 = jnp.float32
BF16 = jnp.bfloat16


def spread(number, start):
    return [(2 * place + start, place) for place in range(number)]


def tile_place(device, spaces):
    plane = spaces.bit_length() - 2
    wide, tall = (plane + 1) // 2, plane // 2
    column = sum(device // 2**src % 2 * 2**dst for src, dst in spread(wide, 0))
    row = sum(device // 2**src % 2 * 2**dst for src, dst in spread(tall, 1))
    layer = device // 2**plane
    return column, row, layer


def tile_owner(column, row, layer, spaces):
    plane = spaces.bit_length() - 2
    wide, tall = (plane + 1) // 2, plane // 2
    owner = layer * 2**plane
    owner = owner + sum(column // 2**dst % 2 * 2**src for src, dst in spread(wide, 0))
    return owner + sum(row // 2**dst % 2 * 2**src for src, dst in spread(tall, 1))


def tile_neighbours(device, spaces):
    plane = spaces.bit_length() - 2
    sizes = (2 ** ((plane + 1) // 2), 2 ** (plane // 2), 2)
    place = tile_place(device, spaces)
    found = []
    for face in range(6):
        dim, step = face // 2, 1 if face % 2 else -1
        moved = list(place)
        moved[dim] = (moved[dim] + step + sizes[dim]) % sizes[dim]
        there = place[dim] < sizes[dim] - 1 if face % 2 else place[dim] > 0
        found.append((there, tile_owner(*moved, spaces)))
    return found


def kernel(
    spaces, reps, reduce_here,
    occ, links, vox, w1, w2, cot,
    out, g1, g2,
    T, U, FB0, FB1, FB2, VX, VH, VG, WA, WB, WC, FI, GA, GB, R, A0, B0, XY, S1, B1, ZR,
    face_send, face_recv, red_send, red_recv,
):
    FB = (FB0, FB1, FB2)
    space, rep = lax.axis_index("space"), lax.axis_index("rep")
    near = tile_neighbours(space, spaces)
    x, z, y, core = space % 2, space // 2, rep // 2, rep % 2

    def core_peer():
        return (space, y * 2 + (1 - core))

    def xy_peer(d):
        flipped_x = 1 - x if d & 1 else x
        flipped_y = 1 - y if d & 2 else y
        return (z * 2 + flipped_x, flipped_y * 2 + core)

    def z_far(d):
        low = 1 - z % 2 if d & 1 else z % 2
        high = 1 - z // 2 if d & 2 else z // 2
        return high * 2 + low

    def z_peer(d):
        return (z_far(d) * 2 + x, rep)

    barrier = pltpu.get_barrier_semaphore()
    if reduce_here:
        peers = [core_peer()] + [xy_peer(d) for d in (1, 2, 3)] + [z_peer(d) for d in (1, 2, 3)]
        for peer in peers:
            pl.semaphore_signal(barrier, inc=1, device_id=peer, device_id_type=MESH)
        pl.semaphore_wait(barrier, 7)
    else:
        total = 0
        for there, owner in near:
            total = total + there.astype(jnp.int32)

            @pl.when(there)
            def _():
                pl.semaphore_signal(barrier, inc=1, device_id=(owner, rep), device_id_type=MESH)

        pl.semaphore_wait(barrier, total)

    def face_copy(field, face):
        return pltpu.make_async_remote_copy(
            src_ref=FB[field].at[OPP[face], pl.ds(0, 4)],
            dst_ref=FB[field].at[OPP[face], pl.ds(4, 4)],
            send_sem=face_send.at[field, face],
            recv_sem=face_recv.at[field, OPP[face]],
            device_id=(near[face][1], rep),
            device_id_type=MESH,
        )

    def arrival(field, face):
        return pltpu.make_async_remote_copy(
            src_ref=FB[field].at[face, pl.ds(0, 4)],
            dst_ref=FB[field].at[face, pl.ds(4, 4)],
            send_sem=face_send.at[field, face],
            recv_sem=face_recv.at[field, face],
            device_id=(near[face][1], rep),
            device_id_type=MESH,
        )

    def send_faces(field):
        for s in range(4):
            cube = T[field, s].reshape(8, 8, 8, 128)
            parts = (
                cube[0].reshape(64, 128), cube[7].reshape(64, 128),
                cube[:, 0].reshape(64, 128), cube[:, 7].reshape(64, 128),
                T[field, s, pl.ds(0, 64, stride=8), :], T[field, s, pl.ds(7, 64, stride=8), :],
            )
            for face, part in enumerate(parts):
                FB[field][OPP[face], s] = part.astype(BF16)
        for face in (4, 5, 2, 3, 0, 1):
            @pl.when(near[face][0])
            def _():
                face_copy(field, face).start()

    def wait_faces(field):
        for face in range(6):
            @pl.when(near[face][0])
            def _():
                arrival(field, face).wait_recv()

    def drain_faces(field):
        for face in range(6):
            @pl.when(near[face][0])
            def _():
                face_copy(field, face).wait_send()

    def halo(field, face, s):
        link = links[s * 6 + face]
        there = link >= 0
        safe = jnp.where(there, link, 0)
        index = safe % 4 + jnp.where(safe // 4 == space, 0, 4)
        index = jnp.where(there, index, 0)
        got = FB[field][face, index].astype(F32)
        return jnp.where(there, got, 0.0)

    level = lax.broadcasted_iota(jnp.int32, (1, 8, 128), 1)

    def down(cube):
        return pltpu.roll(cube, 1, 1)

    def up(cube):
        return pltpu.roll(cube, 7, 1)

    def put_centre(field, V):
        def body(i, carry):
            rows = [T[field, s, pl.ds(pl.multiple_of(i * 64, 64), 64), :].reshape(8, 8, 128) for s in range(4)]
            V[i + 1, 1:9, :, 128:256] = jnp.concatenate(rows, axis=1).astype(BF16)
            return carry

        lax.fori_loop(0, 8, body, 0)

    def put_halos(field, V):
        zero = jnp.zeros((32, 384), BF16)
        for i in (0, 9):
            for j in (0, 9):
                V[i, j] = zero
        for s in range(4):
            cube = T[field, s].reshape(64, 8, 128)
            U[0, s] = down(cube).reshape(512, 128)
            U[1, s] = up(cube).reshape(512, 128)
            U[0, s, pl.ds(0, 64, stride=8), :] = halo(field, 4, s)
            U[1, s, pl.ds(7, 64, stride=8), :] = halo(field, 5, s)

        def body(i, carry):
            for n, lane in ((0, 0), (1, 256)):
                rows = [U[n, s, pl.ds(pl.multiple_of(i * 64, 64), 64), :].reshape(8, 8, 128) for s in range(4)]
                V[i + 1, 1:9, :, lane:lane + 128] = jnp.concatenate(rows, axis=1).astype(BF16)
            return carry

        lax.fori_loop(0, 8, body, 0)
        for face in range(4):
            layers = [halo(field, face, s).reshape(8, 8, 128) for s in range(4)]
            lower = [jnp.where(level == 0, 0.0, down(layer)) for layer in layers]
            upper = [jnp.where(level == 7, 0.0, up(layer)) for layer in layers]
            for lane, group in ((0, lower), (128, layers), (256, upper)):
                value = jnp.concatenate(group, axis=1).astype(BF16)
                edge = 9 if face % 2 else 0
                if face < 2:
                    V[edge, 1:9, :, lane:lane + 128] = value
                else:
                    V[1:9, edge, :, lane:lane + 128] = value

    def convolve(V, W, emit):
        def body(half, carry):
            groups = []
            for p in range(2):
                base = half * 4 + p * 2
                groups.append(jnp.concatenate(
                    [V[base + a, dj:dj + 8].reshape(256, 384) for a in range(4) for dj in range(3)], axis=1
                ))
            both = jnp.concatenate(groups, axis=0)
            total = jnp.dot(both, W[...], preferred_element_type=F32)
            for p in range(2):
                for h in range(2):
                    emit(half * 4 + p * 2 + h, total[p * 256:p * 256 + 256, h * 128:h * 128 + 128])
            return carry

        lax.fori_loop(0, 2, body, 0)

    def weight_product(G, V, which):
        columns = [(dj, dk) for dj in range(3) for dk in range(3)]
        for first in range(0, 9, 2):
            part = columns[first:first + 2]
            right = jnp.concatenate(
                [V[:, dj:dj + 8, :, dk * 128:dk * 128 + 128].reshape(2560, 128) for dj, dk in part], axis=1
            )
            R[which, :, first * 128:(first + len(part)) * 128] = jnp.dot(
                G[...], right, preferred_element_type=F32
            )

    def put_turned(G, i, rows):
        turned = rows.T.astype(BF16)
        for di in range(3):
            at = pl.multiple_of((i + di) * 256, 256)
            G[di * 128:di * 128 + 128, pl.ds(at, 256)] = turned

    def clear_turned(G):
        for di in range(3):
            for i in range(10):
                if not 0 <= i - di < 8:
                    G[di * 128:di * 128 + 128, i * 256:i * 256 + 256] = jnp.zeros((128, 256), BF16)

    def widen(W, source):
        blank = jnp.zeros((1152, 128), BF16)
        for a in range(4):
            W[a * 1152:a * 1152 + 1152, 0:128] = source[a] if a < 3 else blank
            W[a * 1152:a * 1152 + 1152, 128:256] = source[a - 1] if a > 0 else blank

    def widen_back(W, source):
        blank = jnp.zeros((1152, 128), BF16)
        W[3456:4608, 0:128] = blank
        W[0:1152, 128:256] = blank
        for a in range(3):
            for t in range(9):
                turned = source[2 - a, (8 - t) * 128:(8 - t) * 128 + 128, :].T
                W[a * 1152 + t * 128:a * 1152 + t * 128 + 128, 0:128] = turned
                W[(a + 1) * 1152 + t * 128:(a + 1) * 1152 + t * 128 + 128, 128:256] = turned

    def red_copy(which, slot, src, dst, peer):
        return pltpu.make_async_remote_copy(
            src_ref=src, dst_ref=dst, send_sem=red_send.at[which, slot],
            recv_sem=red_recv.at[which, slot], device_id=peer, device_id_type=MESH,
        )

    outs = (g1, g2)
    quarter = y * 2 + x
    my_row = pl.multiple_of(core * 192 + quarter * 48, 16)

    def quarter_of(d):
        return (1 - y if d & 2 else y) * 2 + (1 - x if d & 1 else x)

    def core_copy(w):
        other = pl.multiple_of((1 - core) * 192, 16)
        return red_copy(w, 0, R.at[w, pl.ds(other, 192)], A0.at[w], core_peer())

    def xy_copy(w, d):
        row = pl.multiple_of(quarter_of(d) * 48, 16)
        return red_copy(w, d, B0.at[w, pl.ds(row, 48)], XY.at[w, d - 1], xy_peer(d))

    def z_copy(w, d):
        lane = pl.multiple_of(z_far(d) * 256, 128)
        return red_copy(w, 3 + d, B1.at[w, :, pl.ds(lane, 384)], ZR.at[w, d - 1], z_peer(d))

    def z_back(w, d):
        ref = outs[w].at[pl.ds(my_row, 48), pl.ds(pl.multiple_of(z * 256, 128), 256)]
        return red_copy(w, 6 + d, ref, ref, z_peer(d))

    def z_from(w, d):
        ref = outs[w].at[pl.ds(my_row, 48), pl.ds(pl.multiple_of(z_far(d) * 256, 128), 256)]
        return red_copy(w, 6 + d, ref, ref, z_peer(d))

    def z_last(w, d):
        ref = outs[w].at[pl.ds(my_row, 48), pl.ds(1024, 128)]
        return red_copy(w, 9 + d, ref, ref, z_peer(d))

    def xy_back(w, d, mine):
        q = quarter if mine else quarter_of(d)
        ref = outs[w].at[pl.ds(pl.multiple_of(core * 192 + q * 48, 16), 48)]
        return red_copy(w, 12 + d, ref, ref, xy_peer(d))

    def core_back(w, mine):
        c = core if mine else 1 - core
        ref = outs[w].at[pl.ds(pl.multiple_of(c * 192, 16), 192)]
        return red_copy(w, 16, ref, ref, core_peer())

    D = (1, 2, 3)

    def red_start(w):
        core_copy(w).start()

    def red_xy(w):
        core_copy(w).wait()
        mine = pl.multiple_of(core * 192, 16)
        summed = R[w, pl.ds(mine, 192), :] + A0[w]
        R[w, pl.ds(mine, 192), :] = summed
        B0[w] = summed.astype(BF16)
        for d in (3, 1, 2):
            xy_copy(w, d).start()

    def red_z(w):
        for d in D:
            xy_copy(w, d).wait()
        summed = R[w, pl.ds(my_row, 48), :]
        for d in D:
            summed = summed + XY[w, d - 1].astype(F32)
        S1[w] = summed
        B1[w] = summed.astype(BF16)
        for d in (3, 2, 1):
            z_copy(w, d).start()

    def red_back_z(w):
        for d in D:
            z_copy(w, d).wait()
        summed = S1[w, :, pl.ds(pl.multiple_of(z * 256, 128), 384)]
        for d in D:
            summed = summed + ZR[w, d - 1].astype(F32)
        summed = summed.astype(BF16)
        outs[w][pl.ds(my_row, 48), pl.ds(pl.multiple_of(z * 256, 128), 256)] = summed[:, 0:256]
        for d in (3, 2, 1):
            z_back(w, d).start()

        @pl.when(z == 3)
        def _():
            outs[w][pl.ds(my_row, 48), pl.ds(1024, 128)] = summed[:, 256:384]
            for d in D:
                z_last(w, d).start()

    def red_back_xy(w):
        for d in D:
            z_from(w, d).wait_recv()
            @pl.when(z_far(d) == 3)
            def _():
                z_last(w, d).wait_recv()
        for d in (3, 1, 2):
            xy_back(w, d, True).start()

    def red_back_core(w):
        for d in D:
            xy_back(w, d, False).wait_recv()
        core_back(w, True).start()

    def red_end(w):
        core_back(w, False).wait_recv()
        core_back(w, True).wait_send()
        for d in D:
            xy_back(w, d, True).wait_send()
            z_back(w, d).wait_send()

        @pl.when(z == 3)
        def _():
            for d in D:
                z_last(w, d).wait_send()

    keep = [occ[s].astype(F32) for s in range(4)]
    slot_of = lax.broadcasted_iota(jnp.int32, (32, 128), 0) // 8
    mask = jnp.zeros((32, 128), F32)
    for s in range(4):
        mask = jnp.where(slot_of == s, keep[s], mask)
    mask = mask[None]

    def load(field, source):
        for s in range(4):
            T[field, s] = source[s].astype(F32) * keep[s]

    def masked_rows(rows):
        return (rows.reshape(8, 32, 128) * mask)

    load(0, vox)
    send_faces(0)
    load(1, cot)
    send_faces(1)
    put_centre(0, VX)
    put_centre(1, VG)
    widen(WA, w1)
    widen_back(WB, w2)
    widen(WC, w2)
    clear_turned(GA)
    clear_turned(GB)

    def turn_out(i, carry):
        put_turned(GB, i, VG[i + 1, 1:9, :, 128:256].reshape(256, 128).astype(F32))
        return carry

    lax.fori_loop(0, 8, turn_out, 0)
    wait_faces(0)
    put_halos(0, VX)

    def emit_first(i, rows):
        FI[i] = rows
        hidden = masked_rows(rows * jax.nn.sigmoid(rows))
        for s in range(4):
            T[2, s, pl.ds(pl.multiple_of(i * 64, 64), 64), :] = hidden[:, s * 8:s * 8 + 8].reshape(64, 128)

    convolve(VX, WA, emit_first)
    send_faces(2)
    wait_faces(1)
    put_halos(1, VG)

    def emit_grad(i, rows):
        first = FI[i]
        sigma = jax.nn.sigmoid(first)
        grad = masked_rows(rows * sigma * (1.0 + first * (1.0 - sigma))).reshape(256, 128)
        put_turned(GA, i, grad)

    convolve(VG, WB, emit_grad)
    weight_product(GA, VX, 0)
    if reduce_here:
        red_start(0)
    put_centre(2, VH)
    wait_faces(2)
    put_halos(2, VH)
    if reduce_here:
        red_xy(0)
    weight_product(GB, VH, 1)
    if reduce_here:
        red_start(1)
        red_z(0)

    def emit_out(i, rows):
        inner = VX[i + 1, 1:9, :, 128:256].astype(F32) + rows.reshape(8, 32, 128)
        inner = (inner * mask).astype(BF16).astype(F32)
        for s in range(4):
            out[s, pl.ds(pl.multiple_of(i * 64, 64), 64), :] = inner[:, s * 8:s * 8 + 8].reshape(64, 128).astype(BF16)

    if reduce_here:
        red_xy(1)
        red_back_z(0)
    convolve(VH, WC, emit_out)
    if reduce_here:
        red_z(1)
        red_back_xy(0)
        red_back_z(1)
        red_back_core(0)
        red_back_xy(1)
        red_end(0)
        red_back_core(1)
        red_end(1)
    else:
        g1[...] = R[0]
        g2[...] = R[1]
    for field in range(3):
        drain_faces(field)


def solution(mesh):
    spaces, reps = mesh.shape["space"], mesh.shape["rep"]
    reduce_here = spaces == 8 and reps == 4
    grad_type = BF16 if reduce_here else F32

    def local(voxels, occupied, neighbours, first_weight, second_weight, cotangent):
        smem = pl.BlockSpec(memory_space=pltpu.SMEM)
        vmem = pl.BlockSpec(memory_space=pltpu.VMEM)
        out, first, second = pl.pallas_call(
            functools.partial(kernel, spaces, reps, reduce_here),
            out_shape=(
                jax.ShapeDtypeStruct((4, 512, 128), BF16),
                jax.ShapeDtypeStruct((384, 1152), grad_type),
                jax.ShapeDtypeStruct((384, 1152), grad_type),
            ),
            in_specs=[smem, smem, vmem, vmem, vmem, vmem],
            out_specs=(vmem, vmem, vmem),
            scratch_shapes=[
                pltpu.VMEM((3, 4, 512, 128), F32),
                pltpu.VMEM((2, 4, 512, 128), F32),
                pltpu.VMEM((6, 8, 64, 128), BF16),
                pltpu.VMEM((6, 8, 64, 128), BF16),
                pltpu.VMEM((6, 8, 64, 128), BF16),
                pltpu.VMEM((10, 10, 32, 384), BF16),
                pltpu.VMEM((10, 10, 32, 384), BF16),
                pltpu.VMEM((10, 10, 32, 384), BF16),
                pltpu.VMEM((4608, 256), BF16),
                pltpu.VMEM((4608, 256), BF16),
                pltpu.VMEM((4608, 256), BF16),
                pltpu.VMEM((8, 256, 128), F32),
                pltpu.VMEM((384, 2560), BF16),
                pltpu.VMEM((384, 2560), BF16),
                pltpu.VMEM((2, 384, 1152), F32),
                pltpu.VMEM((2, 192, 1152), F32),
                pltpu.VMEM((2, 192, 1152), BF16),
                pltpu.VMEM((2, 3, 48, 1152), BF16),
                pltpu.VMEM((2, 48, 1152), F32),
                pltpu.VMEM((2, 48, 1152), BF16),
                pltpu.VMEM((2, 3, 48, 384), BF16),
                pltpu.SemaphoreType.DMA((3, 6)),
                pltpu.SemaphoreType.DMA((3, 6)),
                pltpu.SemaphoreType.DMA((2, 17)),
                pltpu.SemaphoreType.DMA((2, 17)),
            ],
            compiler_params=pltpu.CompilerParams(
                collective_id=0, has_side_effects=True, vmem_limit_bytes=56 * 2**20
            ),
            cost_estimate=pl.CostEstimate(flops=9_060_000_000, bytes_accessed=6_000_000, transcendentals=500_000),
        )(
            occupied.reshape(4), neighbours.reshape(24), voxels.reshape(4, 512, 128),
            first_weight.reshape(3, 1152, 128), second_weight.reshape(3, 1152, 128),
            cotangent.reshape(4, 512, 128),
        )
        if not reduce_here:
            first, second = lax.psum((first, second), ("space", "rep"))

        def turned(grad):
            grad = grad.reshape(3, 128, 9, 128).transpose(0, 2, 3, 1)
            return grad.reshape(27, 128, 128).astype(F32)

        return out[None], turned(first), turned(second)

    placed = (
        P("rep", "space", None, None),
        P("rep", "space"),
        P("rep", "space", None),
        P(),
        P(),
        P("rep", "space", None, None),
    )
    return jax.shard_map(
        local,
        mesh=mesh,
        in_specs=placed,
        out_specs=(P("rep", "space", None, None), P(), P()),
        check_vma=False,
    )
```

profile of v0, /device:TPU:0, one launch (start us, length us, event | category | flops | bytes accessed | tf_op | source)
XLA Modules:
  0.0 73.7 jit_solution(4243217591341730582)
XLA Ops:
  0.6 1.3 %reshape.37.links = s32[24]{0:T(128)} reshape(s32[1,4,6]{2,1,0:T(4,128)} %param.8) | data formatting | bytes 192 | tf_op jit(solution)/shard_map/reshape | solution.py:510
  1.9 58.7 %shard_map.85 = (bf16[4,512,128]{2,1,0:T(8,128)(2,1)}, bf16[384,1152]{1,0:T(8,128)(2,1)}, bf16[384,1152]{1,0:T(8,128)(2,1)}) custom-call(s32[4]{0:T(128)} %bitcast.23, s32[24]{0:T(128)} %reshape.37.links, bf16[4,512,128]{2,1,0:T(8,128)(2,1)} %bitcast.21, bf16[3,1152,128]{2,1,0:T(8,128)(2,1)} %bitcast.19, bf16[3,1152,128]{2,1,0:T(8,128)(2,1)} %bitcast.20, ...), custom_call_target="tpu_custom_call" | custom-call | flops 9059999744 | bytes 6000000 | tf_op jit(solution)/shard_map/pallas_call | solution.py:469
  60.6 2.5 %copy.13 = f32[384,1152]{0,1:T(8,128)} copy(bf16[384,1152]{1,0:T(8,128)(2,1)} %get-tuple-element.7) | data formatting | bytes 2654208 | tf_op jit(solution)/shard_map/convert_element_type | solution.py:519
  63.1 2.7 %reshape.44 = f32[3,128,9,128]{1,0,3,2:T(4,128)S(1)} reshape(f32[384,1152]{0,1:T(8,128)} %copy.13) | data formatting | bytes 3538944 | tf_op jit(solution)/shard_map/convert_element_type | solution.py:519
  65.8 0.0 copy-start
  65.8 1.4 %copy.14 = f32[3,9,128,128]{3,2,1,0:T(8,128)} copy(f32[3,9,128,128]{3,0,2,1:T(4,128)S(1)} %bitcast.14) | data formatting | bytes 3538944 | tf_op jit(solution)/shard_map/convert_element_type | solution.py:519
  67.2 0.0 copy-done
  67.2 1.5 %copy.15 = f32[384,1152]{0,1:T(8,128)} copy(bf16[384,1152]{1,0:T(8,128)(2,1)S(1)} %copy-done) | data formatting | bytes 2654208 | tf_op jit(solution)/shard_map/convert_element_type | solution.py:519
  68.7 2.7 %reshape.45 = f32[3,128,9,128]{1,0,3,2:T(4,128)S(1)} reshape(f32[384,1152]{0,1:T(8,128)} %copy.15) | data formatting | bytes 3538944 | tf_op jit(solution)/shard_map/convert_element_type | solution.py:519
  71.4 0.0 copy-start.1
  71.4 1.4 %copy.16 = f32[3,9,128,128]{3,2,1,0:T(8,128)} copy(f32[3,9,128,128]{3,0,2,1:T(4,128)S(1)} %bitcast.15) | data formatting | bytes 3538944 | tf_op jit(solution)/shard_map/convert_element_type | solution.py:519
  72.9 0.0 copy-done.1
  72.9 0.8 %copy.18 = bf16[1,4,512,128]{3,2,1,0:T(8,128)(2,1)} copy(bf16[1,4,512,128]{3,2,1,0:T(8,128)(2,1)S(1)} %bitcast.18) | data formatting | bytes 1048576
Async XLA Ops:
  65.8 1.4 %copy-start = (bf16[384,1152]{1,0:T(8,128)(2,1)S(1)}, bf16[384,1152]{1,0:T(8,128)(2,1)}, u32[]{:S(2)}) copy-start(bf16[384,1152]{1,0:T(8,128)(2,1)} %get-tuple-element.8) | copy-start | bytes 2654212
  71.4 1.4 %copy-start.1 = (bf16[4,512,128]{2,1,0:T(8,128)(2,1)S(1)}, bf16[4,512,128]{2,1,0:T(8,128)(2,1)}, u32[]{:S(2)}) copy-start(bf16[4,512,128]{2,1,0:T(8,128)(2,1)} %get-tuple-element.6) | copy-start | bytes 1572868
where the time goes:
time: 73.9 us; the launch traced here: 73.7 us
  Pallas kernels  58.7 us (79%)
  local copies, waits for them, and re-layouts  14.3 us (19%)
    pallas_call x1, Pallas kernels, local(): pl.pallas_call(functools.partial(kernel, spaces, reps, reduce_here), out_...  58.7 us
    convert_element_type x6, local copies, waits for them, and re-layouts, turned(): return grad.reshape(27, 128, 128).astype(F32)  12.2 us

commit v1 on v0

--- a/solution.py
+++ b/solution.py
@@ -52,7 +52,7 @@
     spaces, reps, reduce_here,
     occ, links, vox, w1, w2, cot,
     out, g1, g2,
-    T, U, FB0, FB1, FB2, VX, VH, VG, WA, WB, WC, FI, GA, GB, R, A0, B0, XY, S1, B1, ZR,
+    T, U, FB0, FB1, FB2, VX, VH, VG, WA, WB, WC, FI, GA, GB, R, A0, B0, XY, S1, B1, ZR, F0, F1,
     face_send, face_recv, red_send, red_recv,
 ):
     FB = (FB0, FB1, FB2)
@@ -141,7 +141,7 @@
                 face_copy(field, face).wait_send()
 
     def halo(field, face, s):
-        link = links[s * 6 + face]
+        link = links[0, s, face]
         there = link >= 0
         safe = jnp.where(there, link, 0)
         index = safe % 4 + jnp.where(safe // 4 == space, 0, 4)
@@ -196,8 +196,10 @@
                 else:
                     V[1:9, edge, :, lane:lane + 128] = value
 
-    def convolve(V, W, emit):
-        def body(half, carry):
+    def convolve(V, W, emit, between=None):
+        for half in range(2):
+            if half and between is not None:
+                between()
             groups = []
             for p in range(2):
                 base = half * 4 + p * 2
@@ -209,13 +211,12 @@
             for p in range(2):
                 for h in range(2):
                     emit(half * 4 + p * 2 + h, total[p * 256:p * 256 + 256, h * 128:h * 128 + 128])
-            return carry
-
-        lax.fori_loop(0, 2, body, 0)
-
-    def weight_product(G, V, which):
+
+    def weight_product(G, V, which, between=None):
         columns = [(dj, dk) for dj in range(3) for dk in range(3)]
         for first in range(0, 9, 2):
+            if first == 4 and between is not None:
+                between()
             part = columns[first:first + 2]
             right = jnp.concatenate(
                 [V[:, dj:dj + 8, :, dk * 128:dk * 128 + 128].reshape(2560, 128) for dj, dk in part], axis=1
@@ -258,7 +259,7 @@
             recv_sem=red_recv.at[which, slot], device_id=peer, device_id_type=MESH,
         )
 
-    outs = (g1, g2)
+    outs = (F0, F1)
     quarter = y * 2 + x
     my_row = pl.multiple_of(core * 192 + quarter * 48, 16)
 
@@ -367,7 +368,7 @@
             for d in D:
                 z_last(w, d).wait_send()
 
-    keep = [occ[s].astype(F32) for s in range(4)]
+    keep = [occ[0, s].astype(F32) for s in range(4)]
     slot_of = lax.broadcasted_iota(jnp.int32, (32, 128), 0) // 8
     mask = jnp.zeros((32, 128), F32)
     for s in range(4):
@@ -380,6 +381,21 @@
 
     def masked_rows(rows):
         return (rows.reshape(8, 32, 128) * mask)
+
+    def nothing():
+        pass
+
+    def when_here(*steps):
+        def run():
+            for step, which in steps:
+                step(which)
+
+        return run if reduce_here else nothing
+
+    def finish(g, source):
+        for di in range(3):
+            for m in range(9):
+                g[di * 9 + m] = source[di * 128:di * 128 + 128, m * 128:m * 128 + 128].T
 
     load(0, vox)
     send_faces(0)
@@ -388,8 +404,6 @@
     put_centre(0, VX)
     put_centre(1, VG)
     widen(WA, w1)
-    widen_back(WB, w2)
-    widen(WC, w2)
     clear_turned(GA)
     clear_turned(GB)
 
@@ -405,12 +419,19 @@
         FI[i] = rows
         hidden = masked_rows(rows * jax.nn.sigmoid(rows))
         for s in range(4):
-            T[2, s, pl.ds(pl.multiple_of(i * 64, 64), 64), :] = hidden[:, s * 8:s * 8 + 8].reshape(64, 128)
+            T[2, s, i * 64:i * 64 + 64, :] = hidden[:, s * 8:s * 8 + 8].reshape(64, 128)
 
     convolve(VX, WA, emit_first)
     send_faces(2)
+    put_centre(2, VH)
+    widen_back(WB, w2)
+    widen(WC, w2)
     wait_faces(1)
     put_halos(1, VG)
+    wait_faces(2)
+    put_halos(2, VH)
+    weight_product(GB, VH, 1)
+    when_here((red_start, 1))()
 
     def emit_grad(i, rows):
         first = FI[i]
@@ -418,42 +439,31 @@
         grad = masked_rows(rows * sigma * (1.0 + first * (1.0 - sigma))).reshape(256, 128)
         put_turned(GA, i, grad)
 
-    convolve(VG, WB, emit_grad)
-    weight_product(GA, VX, 0)
-    if reduce_here:
-        red_start(0)
-    put_centre(2, VH)
-    wait_faces(2)
-    put_halos(2, VH)
-    if reduce_here:
-        red_xy(0)
-    weight_product(GB, VH, 1)
-    if reduce_here:
-        red_start(1)
-        red_z(0)
+    convolve(VG, WB, emit_grad, when_here((red_xy, 1)))
+    weight_product(GA, VX, 0, when_here((red_z, 1)))
+    when_here((red_start, 0))()
 
     def emit_out(i, rows):
         inner = VX[i + 1, 1:9, :, 128:256].astype(F32) + rows.reshape(8, 32, 128)
         inner = (inner * mask).astype(BF16).astype(F32)
         for s in range(4):
-            out[s, pl.ds(pl.multiple_of(i * 64, 64), 64), :] = inner[:, s * 8:s * 8 + 8].reshape(64, 128).astype(BF16)
-
+            out[s, i * 64:i * 64 + 64, :] = inner[:, s * 8:s * 8 + 8].reshape(64, 128).astype(BF16)
+
+    convolve(VH, WC, emit_out, when_here((red_back_z, 1), (red_xy, 0)))
     if reduce_here:
-        red_xy(1)
+        red_back_xy(1)
+        red_z(0)
+        red_back_core(1)
         red_back_z(0)
-    convolve(VH, WC, emit_out)
-    if reduce_here:
-        red_z(1)
+        red_end(1)
         red_back_xy(0)
-        red_back_z(1)
+        finish(g2, F1)
         red_back_core(0)
-        red_back_xy(1)
         red_end(0)
-        red_back_core(1)
-        red_end(1)
+        finish(g1, F0)
     else:
-        g1[...] = R[0]
-        g2[...] = R[1]
+        finish(g1, R.at[0])
+        finish(g2, R.at[1])
     for field in range(3):
         drain_faces(field)
 
@@ -470,8 +480,8 @@
             functools.partial(kernel, spaces, reps, reduce_here),
             out_shape=(
                 jax.ShapeDtypeStruct((4, 512, 128), BF16),
-                jax.ShapeDtypeStruct((384, 1152), grad_type),
-                jax.ShapeDtypeStruct((384, 1152), grad_type),
+                jax.ShapeDtypeStruct((27, 128, 128), grad_type),
+                jax.ShapeDtypeStruct((27, 128, 128), grad_type),
             ),
             in_specs=[smem, smem, vmem, vmem, vmem, vmem],
             out_specs=(vmem, vmem, vmem),
@@ -497,6 +507,8 @@
                 pltpu.VMEM((2, 48, 1152), F32),
                 pltpu.VMEM((2, 48, 1152), BF16),
                 pltpu.VMEM((2, 3, 48, 384), BF16),
+                pltpu.VMEM((384, 1152), BF16),
+                pltpu.VMEM((384, 1152), BF16),
                 pltpu.SemaphoreType.DMA((3, 6)),
                 pltpu.SemaphoreType.DMA((3, 6)),
                 pltpu.SemaphoreType.DMA((2, 17)),
@@ -507,18 +519,14 @@
             ),
             cost_estimate=pl.CostEstimate(flops=9_060_000_000, bytes_accessed=6_000_000, transcendentals=500_000),
         )(
-            occupied.reshape(4), neighbours.reshape(24), voxels.reshape(4, 512, 128),
+            occupied, neighbours, voxels.reshape(4, 512, 128),
             first_weight.reshape(3, 1152, 128), second_weight.reshape(3, 1152, 128),
             cotangent.reshape(4, 512, 128),
         )
         if not reduce_here:
             first, second = lax.psum((first, second), ("space", "rep"))
 
-        def turned(grad):
-            grad = grad.reshape(3, 128, 9, 128).transpose(0, 2, 3, 1)
-            return grad.reshape(27, 128, 128).astype(F32)
-
-        return out[None], turned(first), turned(second)
+        return out[None], first.astype(F32), second.astype(F32)
 
     placed = (
         P("rep", "space", None, None),

time: 73.9 us -> 69.6 us (0.942)
  local copies, waits for them, and re-layouts: 14.3 us -> 0.8 us
  Pallas kernels: 58.7 us -> 63.9 us
  other arithmetic: 0 us -> 4.07 us
    convert_element_type x6 -> x0, local copies, waits for them, and re-layouts: 12.2 us -> none  [turned(): return grad.reshape(27, 128, 128).astype(F32)]
    pallas_call x1, Pallas kernels: 58.7 us -> 63.9 us  [local(): pl.pallas_call(functools.partial(kernel, spaces, reps, reduce_here), out_...]
    convert_element_type x0 -> x2, other arithmetic: none -> 4.07 us  [local(): return (out[None], first.astype(F32), second.astype(F32))]
    reshape x1 -> x0, local copies, waits for them, and re-layouts: 1.27 us -> none  [local(): neighbours.reshape(24)]
where the time goes in v1:
time: 69.6 us; the launch traced here: 69.4 us
  Pallas kernels  63.9 us (92%)
  other arithmetic  4.07 us (6%)
  local copies, waits for them, and re-layouts  0.8 us (1%)
    pallas_call x1, Pallas kernels, local(): pl.pallas_call(functools.partial(kernel, spaces, reps, reduce_here), out_...  63.9 us
    convert_element_type x2, other arithmetic, local(): return (out[None], first.astype(F32), second.astype(F32))  4.07 us

profile of v1, /device:TPU:0, one launch (start us, length us, event | category | flops | bytes accessed | tf_op | source)
XLA Modules:
  0.0 69.4 jit_solution(4609877523129104811)
XLA Ops:
  0.6 63.9 %shard_map.85 = (bf16[4,512,128]{2,1,0:T(8,128)(2,1)}, bf16[27,128,128]{2,1,0:T(8,128)(2,1)}, bf16[27,128,128]{2,1,0:T(8,128)(2,1)}) custom-call(s32[1,4]{1,0:T(1,128)} %occ.1, s32[1,4,6]{2,1,0:T(4,128)} %links.1, bf16[4,512,128]{2,1,0:T(8,128)(2,1)} %bitcast.8, bf16[3,1152,128]{2,1,0:T(8,128)(2,1)} %bitcast.6, bf16[3,1152,128]{2,1,0:T(8,128)(2,1)} %bitcast.7, ...), custom_call_target="tpu_custom_call" | custom-call | flops 9059999744 | bytes 6000000 | tf_op jit(solution)/shard_map/pallas_call | solution.py:479
  64.5 0.0 copy-start
  64.6 2.7 %convert_element_type.6 = f32[27,128,128]{2,1,0:T(8,128)} convert(bf16[27,128,128]{2,1,0:T(8,128)(2,1)} %get-tuple-element.7) | non-fusion elementwise | flops 442368 | bytes 2654208 | tf_op jit(solution)/shard_map/convert_element_type | solution.py:529
  67.2 0.0 copy-done
  67.2 0.0 copy-start.1
  67.2 1.4 %convert_element_type.7 = f32[27,128,128]{2,1,0:T(8,128)} convert(bf16[27,128,128]{2,1,0:T(8,128)(2,1)S(1)} %copy-done) | non-fusion elementwise | flops 442368 | bytes 2654208 | tf_op jit(solution)/shard_map/convert_element_type | solution.py:529
  68.6 0.0 copy-done.1
  68.6 0.8 %copy.10 = bf16[1,4,512,128]{3,2,1,0:T(8,128)(2,1)} copy(bf16[1,4,512,128]{3,2,1,0:T(8,128)(2,1)S(1)} %bitcast.5) | data formatting | bytes 1048576
Async XLA Ops:
  64.5 2.7 %copy-start = (bf16[27,128,128]{2,1,0:T(8,128)(2,1)S(1)}, bf16[27,128,128]{2,1,0:T(8,128)(2,1)}, u32[]{:S(2)}) copy-start(bf16[27,128,128]{2,1,0:T(8,128)(2,1)} %get-tuple-element.8) | copy-start | bytes 2654212
  67.2 1.4 %copy-start.1 = (bf16[4,512,128]{2,1,0:T(8,128)(2,1)S(1)}, bf16[4,512,128]{2,1,0:T(8,128)(2,1)}, u32[]{:S(2)}) copy-start(bf16[4,512,128]{2,1,0:T(8,128)(2,1)} %get-tuple-element.6) | copy-start | bytes 1572868

commit v2 on v1

--- a/solution.py
+++ b/solution.py
@@ -15,6 +15,26 @@
 
 def spread(number, start):
     return [(2 * place + start, place) for place in range(number)]
+
+
+def eye(size):
+    row = lax.broadcasted_iota(jnp.int32, (size, size), 0)
+    column = lax.broadcasted_iota(jnp.int32, (size, size), 1)
+    return (row == column).astype(F32).astype(BF16)
+
+
+def last_by_last(left, right):
+    return lax.dot_general(left, right, (((1,), (1,)), ((), ())), preferred_element_type=F32)
+
+
+def turn_kernel(first, second, g1, g2):
+    for source, g in ((first, g1), (second, g2)):
+        for m in range(0, 9, 2):
+            count = min(2, 9 - m)
+            block = source[:, m * 128:(m + count) * 128]
+            turned = last_by_last(eye(count * 128), block)
+            for n in range(count):
+                g[m + n] = turned[n * 128:n * 128 + 128]
 
 
 def tile_place(device, spaces):
@@ -51,8 +71,8 @@
 def kernel(
     spaces, reps, reduce_here,
     occ, links, vox, w1, w2, cot,
-    out, g1, g2,
-    T, U, FB0, FB1, FB2, VX, VH, VG, WA, WB, WC, FI, GA, GB, R, A0, B0, XY, S1, B1, ZR, F0, F1,
+    out, F0, F1,
+    T, U, FB0, FB1, FB2, VX, VH, VG, WA, WB, WC, FI, GA, GB, R, A0, B0, XA, ZA, SA, BA, XB, ZB, SB, BB,
     face_send, face_recv, red_send, red_recv,
 ):
     FB = (FB0, FB1, FB2)
@@ -196,7 +216,7 @@
                 else:
                     V[1:9, edge, :, lane:lane + 128] = value
 
-    def convolve(V, W, emit, between=None):
+    def convolve(V, W, emit, between=None, back=False):
         for half in range(2):
             if half and between is not None:
                 between()
@@ -207,7 +227,10 @@
                     [V[base + a, dj:dj + 8].reshape(256, 384) for a in range(4) for dj in range(3)], axis=1
                 ))
             both = jnp.concatenate(groups, axis=0)
-            total = jnp.dot(both, W[...], preferred_element_type=F32)
+            if back:
+                total = last_by_last(both, W[...])
+            else:
+                total = jnp.dot(both, W[...], preferred_element_type=F32)
             for p in range(2):
                 for h in range(2):
                     emit(half * 4 + p * 2 + h, total[p * 256:p * 256 + 256, h * 128:h * 128 + 128])
@@ -225,8 +248,10 @@
                 G[...], right, preferred_element_type=F32
             )
 
+    unit = eye(128)
+
     def put_turned(G, i, rows):
-        turned = rows.T.astype(BF16)
+        turned = last_by_last(unit, rows).astype(BF16)
         for di in range(3):
             at = pl.multiple_of((i + di) * 256, 256)
             G[di * 128:di * 128 + 128, pl.ds(at, 256)] = turned
@@ -244,14 +269,15 @@
             W[a * 1152:a * 1152 + 1152, 128:256] = source[a - 1] if a > 0 else blank
 
     def widen_back(W, source):
-        blank = jnp.zeros((1152, 128), BF16)
-        W[3456:4608, 0:128] = blank
-        W[0:1152, 128:256] = blank
+        blank = jnp.zeros((128, 1152), BF16)
+        W[0:128, 3456:4608] = blank
+        W[128:256, 0:1152] = blank
         for a in range(3):
             for t in range(9):
-                turned = source[2 - a, (8 - t) * 128:(8 - t) * 128 + 128, :].T
-                W[a * 1152 + t * 128:a * 1152 + t * 128 + 128, 0:128] = turned
-                W[(a + 1) * 1152 + t * 128:(a + 1) * 1152 + t * 128 + 128, 128:256] = turned
+                piece = source[2 - a, (8 - t) * 128:(8 - t) * 128 + 128, :]
+                lane = a * 1152 + t * 128
+                W[0:128, lane:lane + 128] = piece
+                W[128:256, lane + 1152:lane + 1280] = piece
 
     def red_copy(which, slot, src, dst, peer):
         return pltpu.make_async_remote_copy(
@@ -261,112 +287,177 @@
 
     outs = (F0, F1)
     quarter = y * 2 + x
-    my_row = pl.multiple_of(core * 192 + quarter * 48, 16)
+    D = (1, 2, 3)
+    top = pl.multiple_of(core * 192, 16)
+    low = pl.multiple_of(core * 192 + 128, 16)
+    row_a = pl.multiple_of(core * 192 + quarter * 32, 16)
+    row_b = pl.multiple_of(core * 192 + 128 + quarter * 16, 16)
 
     def quarter_of(d):
         return (1 - y if d & 2 else y) * 2 + (1 - x if d & 1 else x)
+
+    def lanes(place, width):
+        return pl.ds(pl.multiple_of(place * 256, 128), width)
 
     def core_copy(w):
         other = pl.multiple_of((1 - core) * 192, 16)
         return red_copy(w, 0, R.at[w, pl.ds(other, 192)], A0.at[w], core_peer())
 
-    def xy_copy(w, d):
-        row = pl.multiple_of(quarter_of(d) * 48, 16)
-        return red_copy(w, d, B0.at[w, pl.ds(row, 48)], XY.at[w, d - 1], xy_peer(d))
-
-    def z_copy(w, d):
-        lane = pl.multiple_of(z_far(d) * 256, 128)
-        return red_copy(w, 3 + d, B1.at[w, :, pl.ds(lane, 384)], ZR.at[w, d - 1], z_peer(d))
-
-    def z_back(w, d):
-        ref = outs[w].at[pl.ds(my_row, 48), pl.ds(pl.multiple_of(z * 256, 128), 256)]
+    def a_xy(w, d):
+        row = pl.multiple_of(quarter_of(d) * 32, 16)
+        return red_copy(w, d, B0.at[w, pl.ds(row, 32)], XA.at[w, d - 1], xy_peer(d))
+
+    def a_z(w, d):
+        return red_copy(w, 3 + d, BA.at[w, :, lanes(z_far(d), 384)], ZA.at[w, d - 1], z_peer(d))
+
+    def a_back_z(w, d, place):
+        ref = outs[w].at[pl.ds(row_a, 32), lanes(place, 256)]
         return red_copy(w, 6 + d, ref, ref, z_peer(d))
 
-    def z_from(w, d):
-        ref = outs[w].at[pl.ds(my_row, 48), pl.ds(pl.multiple_of(z_far(d) * 256, 128), 256)]
-        return red_copy(w, 6 + d, ref, ref, z_peer(d))
-
-    def z_last(w, d):
-        ref = outs[w].at[pl.ds(my_row, 48), pl.ds(1024, 128)]
+    def a_last_z(w, d):
+        ref = outs[w].at[pl.ds(row_a, 32), pl.ds(1024, 128)]
         return red_copy(w, 9 + d, ref, ref, z_peer(d))
 
-    def xy_back(w, d, mine):
-        q = quarter if mine else quarter_of(d)
-        ref = outs[w].at[pl.ds(pl.multiple_of(core * 192 + q * 48, 16), 48)]
+    def a_back_xy(w, d, q):
+        ref = outs[w].at[pl.ds(pl.multiple_of(core * 192 + q * 32, 16), 32)]
         return red_copy(w, 12 + d, ref, ref, xy_peer(d))
 
-    def core_back(w, mine):
-        c = core if mine else 1 - core
+    def b_z(w, d):
+        return red_copy(w, 15 + d, B0.at[w, pl.ds(128, 64), lanes(z_far(d), 384)], ZB.at[w, d - 1], z_peer(d))
+
+    def b_xy(w, d):
+        row = pl.multiple_of(quarter_of(d) * 16, 16)
+        return red_copy(w, 18 + d, BB.at[w, pl.ds(row, 16)], XB.at[w, d - 1], xy_peer(d))
+
+    def b_rows(q):
+        return pl.ds(pl.multiple_of(core * 192 + 128 + q * 16, 16), 16)
+
+    def b_back_xy(w, d, q):
+        ref = outs[w].at[b_rows(q), lanes(z, 256)]
+        return red_copy(w, 21 + d, ref, ref, xy_peer(d))
+
+    def b_last_xy(w, d, q):
+        ref = outs[w].at[b_rows(q), pl.ds(1024, 128)]
+        return red_copy(w, 24 + d, ref, ref, xy_peer(d))
+
+    def b_back_z(w, d, place):
+        ref = outs[w].at[pl.ds(low, 64), lanes(place, 256)]
+        return red_copy(w, 27 + d, ref, ref, z_peer(d))
+
+    def b_last_z(w, d):
+        ref = outs[w].at[pl.ds(low, 64), pl.ds(1024, 128)]
+        return red_copy(w, 30 + d, ref, ref, z_peer(d))
+
+    def core_back(w, c):
         ref = outs[w].at[pl.ds(pl.multiple_of(c * 192, 16), 192)]
-        return red_copy(w, 16, ref, ref, core_peer())
-
-    D = (1, 2, 3)
+        return red_copy(w, 34, ref, ref, core_peer())
 
     def red_start(w):
         core_copy(w).start()
 
-    def red_xy(w):
+    def red_first(w):
         core_copy(w).wait()
-        mine = pl.multiple_of(core * 192, 16)
-        summed = R[w, pl.ds(mine, 192), :] + A0[w]
-        R[w, pl.ds(mine, 192), :] = summed
+        summed = R[w, pl.ds(top, 192), :] + A0[w]
+        R[w, pl.ds(top, 192), :] = summed
         B0[w] = summed.astype(BF16)
         for d in (3, 1, 2):
-            xy_copy(w, d).start()
-
-    def red_z(w):
-        for d in D:
-            xy_copy(w, d).wait()
-        summed = R[w, pl.ds(my_row, 48), :]
-        for d in D:
-            summed = summed + XY[w, d - 1].astype(F32)
-        S1[w] = summed
-        B1[w] = summed.astype(BF16)
+            a_xy(w, d).start()
+            b_z(w, d).start()
+
+    def red_second(w):
+        for d in D:
+            a_xy(w, d).wait()
+        summed = R[w, pl.ds(row_a, 32), :]
+        for d in D:
+            summed = summed + XA[w, d - 1].astype(F32)
+        SA[w] = summed
+        BA[w] = summed.astype(BF16)
         for d in (3, 2, 1):
-            z_copy(w, d).start()
-
-    def red_back_z(w):
-        for d in D:
-            z_copy(w, d).wait()
-        summed = S1[w, :, pl.ds(pl.multiple_of(z * 256, 128), 384)]
-        for d in D:
-            summed = summed + ZR[w, d - 1].astype(F32)
-        summed = summed.astype(BF16)
-        outs[w][pl.ds(my_row, 48), pl.ds(pl.multiple_of(z * 256, 128), 256)] = summed[:, 0:256]
+            a_z(w, d).start()
+        for d in D:
+            b_z(w, d).wait()
+        summed = R[w, pl.ds(low, 64), lanes(z, 384)]
+        for d in D:
+            summed = summed + ZB[w, d - 1].astype(F32)
+        SB[w] = summed
+        BB[w] = summed.astype(BF16)
+        for d in (3, 1, 2):
+            b_xy(w, d).start()
+
+    def red_third(w):
+        for d in D:
+            a_z(w, d).wait()
+        summed = SA[w, :, lanes(z, 384)]
+        for d in D:
+            summed = summed + ZA[w, d - 1].astype(F32)
+        whole_a = summed.astype(BF16)
+        outs[w][pl.ds(row_a, 32), lanes(z, 256)] = whole_a[:, 0:256]
         for d in (3, 2, 1):
-            z_back(w, d).start()
+            a_back_z(w, d, z).start()
+        for d in D:
+            b_xy(w, d).wait()
+        summed = SB[w, pl.ds(pl.multiple_of(quarter * 16, 16), 16), :]
+        for d in D:
+            summed = summed + XB[w, d - 1].astype(F32)
+        whole_b = summed.astype(BF16)
+        outs[w][pl.ds(row_b, 16), lanes(z, 256)] = whole_b[:, 0:256]
+        for d in (3, 1, 2):
+            b_back_xy(w, d, quarter).start()
 
         @pl.when(z == 3)
         def _():
-            outs[w][pl.ds(my_row, 48), pl.ds(1024, 128)] = summed[:, 256:384]
+            outs[w][pl.ds(row_a, 32), pl.ds(1024, 128)] = whole_a[:, 256:384]
+            outs[w][pl.ds(row_b, 16), pl.ds(1024, 128)] = whole_b[:, 256:384]
             for d in D:
-                z_last(w, d).start()
-
-    def red_back_xy(w):
-        for d in D:
-            z_from(w, d).wait_recv()
+                a_last_z(w, d).start()
+                b_last_xy(w, d, quarter).start()
+
+    def red_fourth(w):
+        for d in D:
+            a_back_z(w, d, z_far(d)).wait_recv()
+
             @pl.when(z_far(d) == 3)
             def _():
-                z_last(w, d).wait_recv()
+                a_last_z(w, d).wait_recv()
         for d in (3, 1, 2):
-            xy_back(w, d, True).start()
-
-    def red_back_core(w):
-        for d in D:
-            xy_back(w, d, False).wait_recv()
-        core_back(w, True).start()
-
-    def red_end(w):
-        core_back(w, False).wait_recv()
-        core_back(w, True).wait_send()
-        for d in D:
-            xy_back(w, d, True).wait_send()
-            z_back(w, d).wait_send()
+            a_back_xy(w, d, quarter).start()
+        for d in D:
+            b_back_xy(w, d, quarter_of(d)).wait_recv()
+        for d in (3, 2, 1):
+            b_back_z(w, d, z).start()
 
         @pl.when(z == 3)
         def _():
             for d in D:
-                z_last(w, d).wait_send()
+                b_last_xy(w, d, quarter_of(d)).wait_recv()
+            for d in D:
+                b_last_z(w, d).start()
+
+    def red_fifth(w):
+        for d in D:
+            a_back_xy(w, d, quarter_of(d)).wait_recv()
+            b_back_z(w, d, z_far(d)).wait_recv()
+
+            @pl.when(z_far(d) == 3)
+            def _():
+                b_last_z(w, d).wait_recv()
+        core_back(w, core).start()
+
+    def red_end(w):
+        core_back(w, 1 - core).wait_recv()
+        core_back(w, core).wait_send()
+        for d in D:
+            a_back_z(w, d, z).wait_send()
+            a_back_xy(w, d, quarter).wait_send()
+            b_back_xy(w, d, quarter).wait_send()
+            b_back_z(w, d, z).wait_send()
+
+        @pl.when(z == 3)
+        def _():
+            for d in D:
+                a_last_z(w, d).wait_send()
+                b_last_xy(w, d, quarter).wait_send()
+                b_last_z(w, d).wait_send()
 
     keep = [occ[0, s].astype(F32) for s in range(4)]
     slot_of = lax.broadcasted_iota(jnp.int32, (32, 128), 0) // 8
@@ -391,11 +482,6 @@
                 step(which)
 
         return run if reduce_here else nothing
-
-    def finish(g, source):
-        for di in range(3):
-            for m in range(9):
-                g[di * 9 + m] = source[di * 128:di * 128 + 128, m * 128:m * 128 + 128].T
 
     load(0, vox)
     send_faces(0)
@@ -408,7 +494,7 @@
     clear_turned(GB)
 
     def turn_out(i, carry):
-        put_turned(GB, i, VG[i + 1, 1:9, :, 128:256].reshape(256, 128).astype(F32))
+        put_turned(GB, i, VG[i + 1, 1:9, :, 128:256].reshape(256, 128))
         return carry
 
     lax.fori_loop(0, 8, turn_out, 0)
@@ -437,10 +523,10 @@
         first = FI[i]
         sigma = jax.nn.sigmoid(first)
         grad = masked_rows(rows * sigma * (1.0 + first * (1.0 - sigma))).reshape(256, 128)
-        put_turned(GA, i, grad)
-
-    convolve(VG, WB, emit_grad, when_here((red_xy, 1)))
-    weight_product(GA, VX, 0, when_here((red_z, 1)))
+        put_turned(GA, i, grad.astype(BF16))
+
+    convolve(VG, WB, emit_grad, when_here((red_first, 1)), True)
+    weight_product(GA, VX, 0, when_here((red_second, 1)))
     when_here((red_start, 0))()
 
     def emit_out(i, rows):
@@ -449,21 +535,19 @@
         for s in range(4):
             out[s, i * 64:i * 64 + 64, :] = inner[:, s * 8:s * 8 + 8].reshape(64, 128).astype(BF16)
 
-    convolve(VH, WC, emit_out, when_here((red_back_z, 1), (red_xy, 0)))
+    convolve(VH, WC, emit_out, when_here((red_third, 1), (red_first, 0)))
     if reduce_here:
-        red_back_xy(1)
-        red_z(0)
-        red_back_core(1)
-        red_back_z(0)
+        red_fourth(1)
+        red_second(0)
+        red_fifth(1)
+        red_third(0)
         red_end(1)
-        red_back_xy(0)
-        finish(g2, F1)
-        red_back_core(0)
+        red_fourth(0)
+        red_fifth(0)
         red_end(0)
-        finish(g1, F0)
     else:
-        finish(g1, R.at[0])
-        finish(g2, R.at[1])
+        F0[...] = R[0]
+        F1[...] = R[1]
     for field in range(3):
         drain_faces(field)
 
@@ -480,8 +564,8 @@
             functools.partial(kernel, spaces, reps, reduce_here),
             out_shape=(
                 jax.ShapeDtypeStruct((4, 512, 128), BF16),
-                jax.ShapeDtypeStruct((27, 128, 128), grad_type),
-                jax.ShapeDtypeStruct((27, 128, 128), grad_type),
+                jax.ShapeDtypeStruct((384, 1152), grad_type),
+                jax.ShapeDtypeStruct((384, 1152), grad_type),
             ),
             in_specs=[smem, smem, vmem, vmem, vmem, vmem],
             out_specs=(vmem, vmem, vmem),
@@ -495,7 +579,7 @@
                 pltpu.VMEM((10, 10, 32, 384), BF16),
                 pltpu.VMEM((10, 10, 32, 384), BF16),
                 pltpu.VMEM((4608, 256), BF16),
-                pltpu.VMEM((4608, 256), BF16),
+                pltpu.VMEM((256, 4608), BF16),
                 pltpu.VMEM((4608, 256), BF16),
                 pltpu.VMEM((8, 256, 128), F32),
                 pltpu.VMEM((384, 2560), BF16),
@@ -503,16 +587,18 @@
                 pltpu.VMEM((2, 384, 1152), F32),
                 pltpu.VMEM((2, 192, 1152), F32),
                 pltpu.VMEM((2, 192, 1152), BF16),
-                pltpu.VMEM((2, 3, 48, 1152), BF16),
-                pltpu.VMEM((2, 48, 1152), F32),
-                pltpu.VMEM((2, 48, 1152), BF16),
-                pltpu.VMEM((2, 3, 48, 384), BF16),
-                pltpu.VMEM((384, 1152), BF16),
-                pltpu.VMEM((384, 1152), BF16),
+                pltpu.VMEM((2, 3, 32, 1152), BF16),
+                pltpu.VMEM((2, 3, 32, 384), BF16),
+                pltpu.VMEM((2, 32, 1152), F32),
+                pltpu.VMEM((2, 32, 1152), BF16),
+                pltpu.VMEM((2, 3, 16, 384), BF16),
+                pltpu.VMEM((2, 3, 64, 384), BF16),
+                pltpu.VMEM((2, 64, 384), F32),
+                pltpu.VMEM((2, 64, 384), BF16),
                 pltpu.SemaphoreType.DMA((3, 6)),
                 pltpu.SemaphoreType.DMA((3, 6)),
-                pltpu.SemaphoreType.DMA((2, 17)),
-                pltpu.SemaphoreType.DMA((2, 17)),
+                pltpu.SemaphoreType.DMA((2, 35)),
+                pltpu.SemaphoreType.DMA((2, 35)),
             ],
             compiler_params=pltpu.CompilerParams(
                 collective_id=0, has_side_effects=True, vmem_limit_bytes=56 * 2**20
@@ -523,10 +609,21 @@
             first_weight.reshape(3, 1152, 128), second_weight.reshape(3, 1152, 128),
             cotangent.reshape(4, 512, 128),
         )
-        if not reduce_here:
-            first, second = lax.psum((first, second), ("space", "rep"))
-
-        return out[None], first.astype(F32), second.astype(F32)
+        if reduce_here:
+            first, second = pl.pallas_call(
+                turn_kernel,
+                grid=(3,),
+                out_shape=[jax.ShapeDtypeStruct((27, 128, 128), F32)] * 2,
+                in_specs=[pl.BlockSpec((128, 1152), lambda i: (i, 0))] * 2,
+                out_specs=[pl.BlockSpec((9, 128, 128), lambda i: (i, 0, 0))] * 2,
+            )(first, second)
+            return out[None], first, second
+        first, second = lax.psum((first, second), ("space", "rep"))
+
+        def turned(grad):
+            return grad.reshape(3, 128, 9, 128).transpose(0, 2, 3, 1).reshape(27, 128, 128)
+
+        return out[None], turned(first), turned(second)
 
     placed = (
         P("rep", "space", None, None),

time: 69.6 us -> 70 us (level)
  Pallas kernels: 63.9 us -> 68.3 us
  other arithmetic: 4.07 us -> 0 us
    pallas_call x0 -> x1, Pallas kernels: none -> 4.42 us  [local(): pl.pallas_call(turn_kernel, grid=(3,), out_shape=[jax.ShapeDtypeStruct((2...]
    convert_element_type x2 -> x0, other arithmetic: 4.07 us -> none  [local(): return (out[None], first.astype(F32), second.astype(F32))]
where the time goes in v2:
time: 70 us; the launch traced here: 69.7 us
  Pallas kernels  68.3 us (98%)
  local copies, waits for them, and re-layouts  0.8 us (1%)
    pallas_call x1, Pallas kernels, local(): pl.pallas_call(functools.partial(kernel, spaces, reps, reduce_here), out_...  63.9 us
    pallas_call x1, Pallas kernels, local(): pl.pallas_call(turn_kernel, grid=(3,), out_shape=[jax.ShapeDtypeStruct((2...  4.42 us

profile of v2, /device:TPU:0, one launch (start us, length us, event | category | flops | bytes accessed | tf_op | source)
XLA Modules:
  0.0 69.7 jit_solution(1365016595482006572)
XLA Ops:
  0.6 63.9 %shard_map.85 = (bf16[4,512,128]{2,1,0:T(8,128)(2,1)}, bf16[384,1152]{1,0:T(8,128)(2,1)}, bf16[384,1152]{1,0:T(8,128)(2,1)}) custom-call(s32[1,4]{1,0:T(1,128)} %occ.1, s32[1,4,6]{2,1,0:T(4,128)} %links.1, bf16[4,512,128]{2,1,0:T(8,128)(2,1)} %bitcast.8, bf16[3,1152,128]{2,1,0:T(8,128)(2,1)} %bitcast.6, bf16[3,1152,128]{2,1,0:T(8,128)(2,1)} %bitcast.7, ...), custom_call_target="tpu_custom_call" | custom-call | flops 9059999744 | bytes 6000000 | tf_op jit(solution)/shard_map/pallas_call | solution.py:563
  64.5 0.0 copy-start
  64.5 4.4 %shard_map.86 = (f32[27,128,128]{2,1,0:T(8,128)}, f32[27,128,128]{2,1,0:T(8,128)}) custom-call(bf16[384,1152]{1,0:T(8,128)(2,1)} %get-tuple-element.9.first, bf16[384,1152]{1,0:T(8,128)(2,1)} %get-tuple-element.10.second), custom_call_target="tpu_custom_call" | custom-call | tf_op jit(solution)/shard_map/pallas_call | solution.py:613
  68.9 0.0 copy-done
  68.9 0.8 %copy.10 = bf16[1,4,512,128]{3,2,1,0:T(8,128)(2,1)} copy(bf16[1,4,512,128]{3,2,1,0:T(8,128)(2,1)S(1)} %bitcast.5) | data formatting | bytes 1048576
Async XLA Ops:
  64.5 4.4 %copy-start = (bf16[4,512,128]{2,1,0:T(8,128)(2,1)S(1)}, bf16[4,512,128]{2,1,0:T(8,128)(2,1)}, u32[]{:S(2)}) copy-start(bf16[4,512,128]{2,1,0:T(8,128)(2,1)} %get-tuple-element.8) | copy-start | bytes 1572868

commit v3 on v2

--- a/solution.py
+++ b/solution.py
@@ -28,13 +28,9 @@
 
 
 def turn_kernel(first, second, g1, g2):
+    unit = eye(384)
     for source, g in ((first, g1), (second, g2)):
-        for m in range(0, 9, 2):
-            count = min(2, 9 - m)
-            block = source[:, m * 128:(m + count) * 128]
-            turned = last_by_last(eye(count * 128), block)
-            for n in range(count):
-                g[m + n] = turned[n * 128:n * 128 + 128]
+        g[...] = last_by_last(unit, source[...]).reshape(3, 128, 128)
 
 
 def tile_place(device, spaces):
@@ -235,17 +231,15 @@
                 for h in range(2):
                     emit(half * 4 + p * 2 + h, total[p * 256:p * 256 + 256, h * 128:h * 128 + 128])
 
-    def weight_product(G, V, which, between=None):
+    def weight_product(G, V, which, start, count):
         columns = [(dj, dk) for dj in range(3) for dk in range(3)]
         for first in range(0, 9, 2):
-            if first == 4 and between is not None:
-                between()
             part = columns[first:first + 2]
             right = jnp.concatenate(
                 [V[:, dj:dj + 8, :, dk * 128:dk * 128 + 128].reshape(2560, 128) for dj, dk in part], axis=1
             )
-            R[which, :, first * 128:(first + len(part)) * 128] = jnp.dot(
-                G[...], right, preferred_element_type=F32
+            R[which, pl.ds(start, count), first * 128:(first + len(part)) * 128] = jnp.dot(
+                G[pl.ds(start, count), :], right, preferred_element_type=F32
             )
 
     unit = eye(128)
@@ -473,16 +467,6 @@
     def masked_rows(rows):
         return (rows.reshape(8, 32, 128) * mask)
 
-    def nothing():
-        pass
-
-    def when_here(*steps):
-        def run():
-            for step, which in steps:
-                step(which)
-
-        return run if reduce_here else nothing
-
     load(0, vox)
     send_faces(0)
     load(1, cot)
@@ -514,10 +498,6 @@
     widen(WC, w2)
     wait_faces(1)
     put_halos(1, VG)
-    wait_faces(2)
-    put_halos(2, VH)
-    weight_product(GB, VH, 1)
-    when_here((red_start, 1))()
 
     def emit_grad(i, rows):
         first = FI[i]
@@ -525,27 +505,45 @@
         grad = masked_rows(rows * sigma * (1.0 + first * (1.0 - sigma))).reshape(256, 128)
         put_turned(GA, i, grad.astype(BF16))
 
-    convolve(VG, WB, emit_grad, when_here((red_first, 1)), True)
-    weight_product(GA, VX, 0, when_here((red_second, 1)))
-    when_here((red_start, 0))()
-
     def emit_out(i, rows):
         inner = VX[i + 1, 1:9, :, 128:256].astype(F32) + rows.reshape(8, 32, 128)
         inner = (inner * mask).astype(BF16).astype(F32)
         for s in range(4):
             out[s, i * 64:i * 64 + 64, :] = inner[:, s * 8:s * 8 + 8].reshape(64, 128).astype(BF16)
 
-    convolve(VH, WC, emit_out, when_here((red_third, 1), (red_first, 0)))
+    convolve(VG, WB, emit_grad, None, True)
     if reduce_here:
+        away = pl.multiple_of((1 - core) * 192, 16)
+        weight_product(GA, VX, 0, away, 192)
+        red_start(0)
+        weight_product(GA, VX, 0, top, 192)
+        red_first(0)
+        wait_faces(2)
+        put_halos(2, VH)
+        weight_product(GB, VH, 1, away, 192)
+        red_start(1)
+        red_second(0)
+        weight_product(GB, VH, 1, top, 192)
+        red_first(1)
+        red_third(0)
+
+        def between():
+            red_second(1)
+            red_fourth(0)
+
+        convolve(VH, WC, emit_out, between)
+        red_third(1)
+        red_fifth(0)
         red_fourth(1)
-        red_second(0)
+        red_end(0)
         red_fifth(1)
-        red_third(0)
         red_end(1)
-        red_fourth(0)
-        red_fifth(0)
-        red_end(0)
     else:
+        weight_product(GA, VX, 0, 0, 384)
+        wait_faces(2)
+        put_halos(2, VH)
+        weight_product(GB, VH, 1, 0, 384)
+        convolve(VH, WC, emit_out)
         F0[...] = R[0]
         F1[...] = R[1]
     for field in range(3):
@@ -612,10 +610,10 @@
         if reduce_here:
             first, second = pl.pallas_call(
                 turn_kernel,
-                grid=(3,),
+                grid=(3, 3),
                 out_shape=[jax.ShapeDtypeStruct((27, 128, 128), F32)] * 2,
-                in_specs=[pl.BlockSpec((128, 1152), lambda i: (i, 0))] * 2,
-                out_specs=[pl.BlockSpec((9, 128, 128), lambda i: (i, 0, 0))] * 2,
+                in_specs=[pl.BlockSpec((128, 384), lambda i, j: (i, j))] * 2,
+                out_specs=[pl.BlockSpec((3, 128, 128), lambda i, j: (i * 3 + j, 0, 0))] * 2,
             )(first, second)
             return out[None], first, second
         first, second = lax.psum((first, second), ("space", "rep"))

time: 70 us -> 68.9 us (0.984)
  Pallas kernels: 68.3 us -> 67 us
    pallas_call x1, Pallas kernels: 63.9 us -> 59.5 us  [local(): pl.pallas_call(functools.partial(kernel, spaces, reps, reduce_here), out_...]
    pallas_call x1, Pallas kernels: 4.42 us -> 7.53 us  [local(): pl.pallas_call(turn_kernel, grid=(3, 3), out_shape=[jax.ShapeDtypeStruct(...]
where the time goes in v3:
time: 68.9 us; the launch traced here: 68.5 us
  Pallas kernels  67 us (97%)
  local copies, waits for them, and re-layouts  0.8 us (1%)
    pallas_call x1, Pallas kernels, local(): pl.pallas_call(functools.partial(kernel, spaces, reps, reduce_here), out_...  59.5 us
    pallas_call x1, Pallas kernels, local(): pl.pallas_call(turn_kernel, grid=(3, 3), out_shape=[jax.ShapeDtypeStruct(...  7.53 us

profile of v3, /device:TPU:0, one launch (start us, length us, event | category | flops | bytes accessed | tf_op | source)
XLA Modules:
  0.0 68.5 jit_solution(10621606510870963427)
XLA Ops:
  0.6 59.5 %shard_map.85 = (bf16[4,512,128]{2,1,0:T(8,128)(2,1)}, bf16[384,1152]{1,0:T(8,128)(2,1)}, bf16[384,1152]{1,0:T(8,128)(2,1)}) custom-call(s32[1,4]{1,0:T(1,128)} %occ.1, s32[1,4,6]{2,1,0:T(4,128)} %links.1, bf16[4,512,128]{2,1,0:T(8,128)(2,1)} %bitcast.8, bf16[3,1152,128]{2,1,0:T(8,128)(2,1)} %bitcast.6, bf16[3,1152,128]{2,1,0:T(8,128)(2,1)} %bitcast.7, ...), custom_call_target="tpu_custom_call" | custom-call | flops 9059999744 | bytes 6000000 | tf_op jit(solution)/shard_map/pallas_call | solution.py:561
  60.1 0.0 copy-start
  60.1 7.5 %shard_map.86 = (f32[27,128,128]{2,1,0:T(8,128)}, f32[27,128,128]{2,1,0:T(8,128)}) custom-call(bf16[384,1152]{1,0:T(8,128)(2,1)} %get-tuple-element.9.first, bf16[384,1152]{1,0:T(8,128)(2,1)} %get-tuple-element.10.second), custom_call_target="tpu_custom_call" | custom-call | tf_op jit(solution)/shard_map/pallas_call | solution.py:611
  67.7 0.0 copy-done
  67.7 0.8 %copy.10 = bf16[1,4,512,128]{3,2,1,0:T(8,128)(2,1)} copy(bf16[1,4,512,128]{3,2,1,0:T(8,128)(2,1)S(1)} %bitcast.5) | data formatting | bytes 1048576
Async XLA Ops:
  60.1 7.5 %copy-start = (bf16[4,512,128]{2,1,0:T(8,128)(2,1)S(1)}, bf16[4,512,128]{2,1,0:T(8,128)(2,1)}, u32[]{:S(2)}) copy-start(bf16[4,512,128]{2,1,0:T(8,128)(2,1)} %get-tuple-element.8) | copy-start | bytes 1572868

commit v4 on v3

--- a/solution.py
+++ b/solution.py
@@ -27,10 +27,17 @@
     return lax.dot_general(left, right, (((1,), (1,)), ((), ())), preferred_element_type=F32)
 
 
+def turn(source, g, base):
+    for m in range(0, 9, 2):
+        count = min(2, 9 - m)
+        turned = last_by_last(eye(count * 128), source[:, m * 128:(m + count) * 128])
+        for n in range(count):
+            g[base + m + n] = turned[n * 128:n * 128 + 128].astype(g.dtype)
+
+
 def turn_kernel(first, second, g1, g2):
-    unit = eye(384)
-    for source, g in ((first, g1), (second, g2)):
-        g[...] = last_by_last(unit, source[...]).reshape(3, 128, 128)
+    g1[...] = first[...].astype(F32)
+    turn(second, g2, 0)
 
 
 def tile_place(device, spaces):
@@ -67,8 +74,8 @@
 def kernel(
     spaces, reps, reduce_here,
     occ, links, vox, w1, w2, cot,
-    out, F0, F1,
-    T, U, FB0, FB1, FB2, VX, VH, VG, WA, WB, WC, FI, GA, GB, R, A0, B0, XA, ZA, SA, BA, XB, ZB, SB, BB,
+    out, g1, F1,
+    T, U, FB0, FB1, FB2, VX, VH, VG, WA, WB, WC, FI, GA, GB, R, A0, B0, XA, ZA, SA, BA, XB, ZB, SB, BB, F0,
     face_send, face_recv, red_send, red_recv,
 ):
     FB = (FB0, FB1, FB2)
@@ -212,7 +219,7 @@
                 else:
                     V[1:9, edge, :, lane:lane + 128] = value
 
-    def convolve(V, W, emit, between=None, back=False):
+    def convolve(V, W, emit, between=None):
         for half in range(2):
             if half and between is not None:
                 between()
@@ -223,10 +230,7 @@
                     [V[base + a, dj:dj + 8].reshape(256, 384) for a in range(4) for dj in range(3)], axis=1
                 ))
             both = jnp.concatenate(groups, axis=0)
-            if back:
-                total = last_by_last(both, W[...])
-            else:
-                total = jnp.dot(both, W[...], preferred_element_type=F32)
+            total = jnp.dot(both, W[...], preferred_element_type=F32)
             for p in range(2):
                 for h in range(2):
                     emit(half * 4 + p * 2 + h, total[p * 256:p * 256 + 256, h * 128:h * 128 + 128])
@@ -263,15 +267,15 @@
             W[a * 1152:a * 1152 + 1152, 128:256] = source[a - 1] if a > 0 else blank
 
     def widen_back(W, source):
-        blank = jnp.zeros((128, 1152), BF16)
-        W[0:128, 3456:4608] = blank
-        W[128:256, 0:1152] = blank
+        blank = jnp.zeros((1152, 128), BF16)
+        W[3456:4608, 0:128] = blank
+        W[0:1152, 128:256] = blank
         for a in range(3):
             for t in range(9):
-                piece = source[2 - a, (8 - t) * 128:(8 - t) * 128 + 128, :]
-                lane = a * 1152 + t * 128
-                W[0:128, lane:lane + 128] = piece
-                W[128:256, lane + 1152:lane + 1280] = piece
+                turned = source[2 - a, (8 - t) * 128:(8 - t) * 128 + 128, :].T
+                row = a * 1152 + t * 128
+                W[row:row + 128, 0:128] = turned
+                W[row + 1152:row + 1280, 128:256] = turned
 
     def red_copy(which, slot, src, dst, peer):
         return pltpu.make_async_remote_copy(
@@ -511,7 +515,7 @@
         for s in range(4):
             out[s, i * 64:i * 64 + 64, :] = inner[:, s * 8:s * 8 + 8].reshape(64, 128).astype(BF16)
 
-    convolve(VG, WB, emit_grad, None, True)
+    convolve(VG, WB, emit_grad)
     if reduce_here:
         away = pl.multiple_of((1 - core) * 192, 16)
         weight_product(GA, VX, 0, away, 192)
@@ -536,6 +540,8 @@
         red_fifth(0)
         red_fourth(1)
         red_end(0)
+        for di in range(3):
+            turn(F0.at[pl.ds(di * 128, 128)], g1, di * 9)
         red_fifth(1)
         red_end(1)
     else:
@@ -544,7 +550,7 @@
         put_halos(2, VH)
         weight_product(GB, VH, 1, 0, 384)
         convolve(VH, WC, emit_out)
-        F0[...] = R[0]
+        g1[...] = R[0]
         F1[...] = R[1]
     for field in range(3):
         drain_faces(field)
@@ -562,7 +568,7 @@
             functools.partial(kernel, spaces, reps, reduce_here),
             out_shape=(
                 jax.ShapeDtypeStruct((4, 512, 128), BF16),
-                jax.ShapeDtypeStruct((384, 1152), grad_type),
+                jax.ShapeDtypeStruct((27, 128, 128) if reduce_here else (384, 1152), grad_type),
                 jax.ShapeDtypeStruct((384, 1152), grad_type),
             ),
             in_specs=[smem, smem, vmem, vmem, vmem, vmem],
@@ -577,7 +583,7 @@
                 pltpu.VMEM((10, 10, 32, 384), BF16),
                 pltpu.VMEM((10, 10, 32, 384), BF16),
                 pltpu.VMEM((4608, 256), BF16),
-                pltpu.VMEM((256, 4608), BF16),
+                pltpu.VMEM((4608, 256), BF16),
                 pltpu.VMEM((4608, 256), BF16),
                 pltpu.VMEM((8, 256, 128), F32),
                 pltpu.VMEM((384, 2560), BF16),
@@ -593,6 +599,7 @@
                 pltpu.VMEM((2, 3, 64, 384), BF16),
                 pltpu.VMEM((2, 64, 384), F32),
                 pltpu.VMEM((2, 64, 384), BF16),
+                pltpu.VMEM((384, 1152), grad_type),
                 pltpu.SemaphoreType.DMA((3, 6)),
                 pltpu.SemaphoreType.DMA((3, 6)),
                 pltpu.SemaphoreType.DMA((2, 35)),
@@ -610,10 +617,13 @@
         if reduce_here:
             first, second = pl.pallas_call(
                 turn_kernel,
-                grid=(3, 3),
+                grid=(3,),
                 out_shape=[jax.ShapeDtypeStruct((27, 128, 128), F32)] * 2,
-                in_specs=[pl.BlockSpec((128, 384), lambda i, j: (i, j))] * 2,
-                out_specs=[pl.BlockSpec((3, 128, 128), lambda i, j: (i * 3 + j, 0, 0))] * 2,
+                in_specs=[
+                    pl.BlockSpec((9, 128, 128), lambda i: (i, 0, 0)),
+                    pl.BlockSpec((128, 1152), lambda i: (i, 0)),
+                ],
+                out_specs=[pl.BlockSpec((9, 128, 128), lambda i: (i, 0, 0))] * 2,
             )(first, second)
             return out[None], first, second
         first, second = lax.psum((first, second), ("space", "rep"))

time: 68.9 us -> 64.9 us (0.942)
  Pallas kernels: 67 us -> 63.2 us
    pallas_call x1, Pallas kernels: 7.53 us -> 4.2 us  [local(): pl.pallas_call(turn_kernel, grid=(3,), out_shape=[jax.ShapeDtypeStruct((2...]
where the time goes in v4:
time: 64.9 us; the launch traced here: 64.6 us
  Pallas kernels  63.2 us (97%)
  local copies, waits for them, and re-layouts  0.8 us (1%)
  between operations  0.65 us (1%)
    pallas_call x1, Pallas kernels, local(): pl.pallas_call(functools.partial(kernel, spaces, reps, reduce_here), out_...  59 us
    pallas_call x1, Pallas kernels, local(): pl.pallas_call(turn_kernel, grid=(3,), out_shape=[jax.ShapeDtypeStruct((2...  4.2 us

profile of v4, /device:TPU:0, one launch (start us, length us, event | category | flops | bytes accessed | tf_op | source)
XLA Modules:
  0.0 64.6 jit_solution(3041811385335053359)
XLA Ops:
  0.6 59.0 %shard_map.85 = (bf16[4,512,128]{2,1,0:T(8,128)(2,1)}, bf16[27,128,128]{2,1,0:T(8,128)(2,1)}, bf16[384,1152]{1,0:T(8,128)(2,1)}) custom-call(s32[1,4]{1,0:T(1,128)} %occ.1, s32[1,4,6]{2,1,0:T(4,128)} %links.1, bf16[4,512,128]{2,1,0:T(8,128)(2,1)} %bitcast.8, bf16[3,1152,128]{2,1,0:T(8,128)(2,1)} %bitcast.6, bf16[3,1152,128]{2,1,0:T(8,128)(2,1)} %bitcast.7, ...), custom_call_target="tpu_custom_call" | custom-call | flops 9059999744 | bytes 6000000 | tf_op jit(solution)/shard_map/pallas_call | solution.py:567
  59.6 0.0 copy-start
  59.6 4.2 %shard_map.86 = (f32[27,128,128]{2,1,0:T(8,128)}, f32[27,128,128]{2,1,0:T(8,128)}) custom-call(bf16[27,128,128]{2,1,0:T(8,128)(2,1)} %get-tuple-element.9.first, bf16[384,1152]{1,0:T(8,128)(2,1)} %get-tuple-element.10.second), custom_call_target="tpu_custom_call" | custom-call | tf_op jit(solution)/shard_map/pallas_call | solution.py:618
  63.8 0.0 copy-done
  63.9 0.8 %copy.10 = bf16[1,4,512,128]{3,2,1,0:T(8,128)(2,1)} copy(bf16[1,4,512,128]{3,2,1,0:T(8,128)(2,1)S(1)} %bitcast.5) | data formatting | bytes 1048576
Async XLA Ops:
  59.6 4.2 %copy-start = (bf16[4,512,128]{2,1,0:T(8,128)(2,1)S(1)}, bf16[4,512,128]{2,1,0:T(8,128)(2,1)}, u32[]{:S(2)}) copy-start(bf16[4,512,128]{2,1,0:T(8,128)(2,1)} %get-tuple-element.8) | copy-start | bytes 1572868

commit v5 on v4

--- a/solution.py
+++ b/solution.py
@@ -517,25 +517,22 @@
 
     convolve(VG, WB, emit_grad)
     if reduce_here:
-        away = pl.multiple_of((1 - core) * 192, 16)
-        weight_product(GA, VX, 0, away, 192)
+        weight_product(GA, VX, 0, 0, 384)
         red_start(0)
-        weight_product(GA, VX, 0, top, 192)
-        red_first(0)
         wait_faces(2)
         put_halos(2, VH)
-        weight_product(GB, VH, 1, away, 192)
+        red_first(0)
+        weight_product(GB, VH, 1, 0, 384)
         red_start(1)
         red_second(0)
-        weight_product(GB, VH, 1, top, 192)
-        red_first(1)
-        red_third(0)
 
         def between():
-            red_second(1)
-            red_fourth(0)
+            red_first(1)
+            red_third(0)
 
         convolve(VH, WC, emit_out, between)
+        red_second(1)
+        red_fourth(0)
         red_third(1)
         red_fifth(0)
         red_fourth(1)

time: 64.9 us -> 68 us (1.048)
  Pallas kernels: 63.2 us -> 66.3 us
    pallas_call x1, Pallas kernels: 59 us -> 62.1 us  [local(): pl.pallas_call(functools.partial(kernel, spaces, reps, reduce_here), out_...]
where the time goes in v5:
time: 68 us; the launch traced here: 67.8 us
  Pallas kernels  66.3 us (98%)
  local copies, waits for them, and re-layouts  0.8 us (1%)
    pallas_call x1, Pallas kernels, local(): pl.pallas_call(functools.partial(kernel, spaces, reps, reduce_here), out_...  62.1 us
    pallas_call x1, Pallas kernels, local(): pl.pallas_call(turn_kernel, grid=(3,), out_shape=[jax.ShapeDtypeStruct((2...  4.2 us

profile of v5, /device:TPU:0, one launch (start us, length us, event | category | flops | bytes accessed | tf_op | source)
XLA Modules:
  0.0 67.8 jit_solution(13201162786608842226)
XLA Ops:
  0.6 62.1 %shard_map.85 = (bf16[4,512,128]{2,1,0:T(8,128)(2,1)}, bf16[27,128,128]{2,1,0:T(8,128)(2,1)}, bf16[384,1152]{1,0:T(8,128)(2,1)}) custom-call(s32[1,4]{1,0:T(1,128)} %occ.1, s32[1,4,6]{2,1,0:T(4,128)} %links.1, bf16[4,512,128]{2,1,0:T(8,128)(2,1)} %bitcast.8, bf16[3,1152,128]{2,1,0:T(8,128)(2,1)} %bitcast.6, bf16[3,1152,128]{2,1,0:T(8,128)(2,1)} %bitcast.7, ...), custom_call_target="tpu_custom_call" | custom-call | flops 9059999744 | bytes 6000000 | tf_op jit(solution)/shard_map/pallas_call | solution.py:564
  62.7 0.0 copy-start
  62.8 4.2 %shard_map.86 = (f32[27,128,128]{2,1,0:T(8,128)}, f32[27,128,128]{2,1,0:T(8,128)}) custom-call(bf16[27,128,128]{2,1,0:T(8,128)(2,1)} %get-tuple-element.9.first, bf16[384,1152]{1,0:T(8,128)(2,1)} %get-tuple-element.10.second), custom_call_target="tpu_custom_call" | custom-call | tf_op jit(solution)/shard_map/pallas_call | solution.py:615
  67.0 0.0 copy-done
  67.0 0.8 %copy.10 = bf16[1,4,512,128]{3,2,1,0:T(8,128)(2,1)} copy(bf16[1,4,512,128]{3,2,1,0:T(8,128)(2,1)S(1)} %bitcast.5) | data formatting | bytes 1048576
Async XLA Ops:
  62.7 4.2 %copy-start = (bf16[4,512,128]{2,1,0:T(8,128)(2,1)S(1)}, bf16[4,512,128]{2,1,0:T(8,128)(2,1)}, u32[]{:S(2)}) copy-start(bf16[4,512,128]{2,1,0:T(8,128)(2,1)} %get-tuple-element.8) | copy-start | bytes 1572868
